TPU v7x, 128 devices: a whole 4x4x4 slice. The times are simulated.
128 devices in a mesh: pop: 4 (over y_hi, core), tp: 16 (over z, x), pp: 2 (over y_lo).
Axes of the slice: x: 4, y: 4 (y_hi: 2, y_lo: 2; y = y_hi * 2 + y_lo), z: 4, core: 2. Of those that a mesh axis runs over, the one named last changes fastest.
Arguments:
- hidden_in: bfloat16 [256, 8, 4096], P('tp', 'pop'), may hold values from -6 to 6
- norm_gain: float32 [2, 4096], P('pp'), may hold values from 0.5 to 1.5
- w_gate: bfloat16 [2, 4096, 12288], P('pp', None, 'tp'), may hold values from -0.09375 to 0.09375
- w_up: bfloat16 [2, 4096, 12288], P('pp', None, 'tp'), may hold values from -0.09375 to 0.09375
- w_down: bfloat16 [2, 12288, 4096], P('pp', 'tp'), may hold values from -0.0546875 to 0.0546875
- gate_left: bfloat16 [2, 8, 4096], P('pp', 'pop'), may hold values from -6 to 6
- gate_right: bfloat16 [2, 8, 12288], P('pp', 'pop', 'tp'), may hold values from -6 to 6
- up_left: bfloat16 [2, 8, 4096], P('pp', 'pop'), may hold values from -6 to 6
- up_right: bfloat16 [2, 8, 12288], P('pp', 'pop', 'tp'), may hold values from -6 to 6
- down_left: bfloat16 [2, 8, 12288], P('pp', 'pop', 'tp'), may hold values from -6 to 6
- down_right: bfloat16 [2, 8, 4096], P('pp', 'pop'), may hold values from -6 to 6
- ranks: int32 [8], P('pop'), may hold values from 0 to 7, each once
Outputs:
- section_out: bfloat16 [2, 256, 8, 4096], P('pp', 'tp', 'pop')
- update_gate: bfloat16 [2, 4096, 12288], P('pp', 'pop', 'tp')
- update_up: bfloat16 [2, 4096, 12288], P('pp', 'pop', 'tp')
- update_down: bfloat16 [2, 12288, 4096], P('pp', 'tp', 'pop')
Inputs may be any that keep to these rules, and one draw needn't show every extreme that they name: `ranks`: each number from 0 to 7 is the rank of exactly one member.
All inputs are finite; a program needn't handle non-finite values.
Results may differ from a plain program's by a relative error of at most 0.014.
Values may be sent and summed in bfloat16 or wider, within the bound.
No kernel may reach another device: no remote copies, remote signals or barrier semaphores. Data moves between devices by JAX's collectives and lax.ppermute only.
A program may use at most 128 MiB of HBM per device.

v0:
```python
import math
import jax
import jax.numpy as jnp
from jax import lax
from jax.sharding import PartitionSpec as P

sigma_scale = 0.3
norm_eps = 1e-05


def from_behind(block, axis, distance):
    devices = range(lax.axis_size(axis))
    route = [(i - distance, i) for i in devices if i - distance in devices]
    return lax.ppermute(block, axis, route)


def sent_together(arrays, axis, dim, along):
    both = jnp.concatenate(arrays, axis=along)
    out, at, done = (lax.all_gather(both, axis, axis=dim, tiled=True), 0, [])
    for a in arrays:
        done.append(lax.slice_in_dim(out, at, at + a.shape[along], axis=along))
        at += a.shape[along]
    return tuple(done)


def feed_forward(
    block,
    gain,
    w_gate,
    w_up,
    w_down,
    gate_left,
    gate_right,
    up_left,
    up_right,
    down_left,
    down_right,
):
    values = block.astype(jnp.float32)
    mean_sq = jnp.mean(values * values, axis=-1, keepdims=True)
    normed = (values * lax.rsqrt(mean_sq + norm_eps) * gain).astype(jnp.bfloat16)
    coef_in = sigma_scale / math.sqrt(block.shape[-1])
    coef_hidden = sigma_scale / math.sqrt(w_gate.shape[-1] * lax.axis_size("tp"))
    gate_wide = gate_right.astype(jnp.float32)[None]
    up_wide = up_right.astype(jnp.float32)[None]
    down_wide = down_right.astype(jnp.float32)[None]
    piece = lax.all_gather(normed, "tp", axis=0, tiled=True)
    gate = jnp.einsum("rkd,df->rkf", piece, w_gate, preferred_element_type=jnp.float32)
    gate_side = jnp.einsum("rkd,kd->rk", piece, gate_left, preferred_element_type=jnp.float32)
    gate = gate + coef_in * gate_side[:, :, None] * gate_wide
    upper = jnp.einsum("rkd,df->rkf", piece, w_up, preferred_element_type=jnp.float32)
    up_side = jnp.einsum("rkd,kd->rk", piece, up_left, preferred_element_type=jnp.float32)
    upper = upper + coef_in * up_side[:, :, None] * up_wide
    inner = (jax.nn.silu(gate) * upper).astype(jnp.bfloat16)
    term = jnp.einsum("rkf,fd->rkd", inner, w_down, preferred_element_type=jnp.float32)
    down_side = jnp.einsum("rkf,kf->rk", inner, down_left, preferred_element_type=jnp.float32)
    summed = lax.psum_scatter(
        (term + coef_hidden * down_side[:, :, None] * down_wide).astype(jnp.bfloat16),
        "tp",
        scatter_dimension=0,
        tiled=True,
    ).astype(jnp.float32)
    return (values + summed).astype(jnp.bfloat16)


def grouped_outer(fitness, left, right, groups):
    weighted = (fitness[:, None] * left.astype(jnp.float32)).reshape(groups, -1, left.shape[1])
    other = right.astype(jnp.float32).reshape(groups, -1, right.shape[1])
    parts = jnp.einsum("gmi,gmj->gij", weighted, other)
    rounded = lax.optimization_barrier(parts.astype(jnp.bfloat16)).astype(jnp.float32)
    return jnp.sum(rounded, axis=0)


def per_device(
    hidden_in,
    norm_gain,
    w_gate,
    w_up,
    w_down,
    gate_left,
    gate_right,
    up_left,
    up_right,
    down_left,
    down_right,
    ranks,
):
    seq_rows, members, width = hidden_in.shape
    sections = lax.axis_size("pp")
    section_index = lax.axis_index("pp")
    gain = norm_gain[0]
    gate_weight = w_gate[0]
    up_weight = w_up[0]
    down_weight = w_down[0]
    vectors = [gate_left[0], gate_right[0], up_left[0], up_right[0], down_left[0], down_right[0]]
    block_list = [(0, 0)]
    block_count = len(block_list)
    ticks = block_count + sections - 1
    output = jnp.zeros_like(hidden_in)
    arrived = jnp.zeros((seq_rows, members, width), jnp.bfloat16)
    for tick in range(ticks):
        if tick < block_count:
            own = hidden_in
        else:
            own = jnp.zeros_like(arrived)
        current = jnp.where(section_index == 0, own, arrived)
        position = tick - section_index
        picked = [vector for vector in vectors]
        result = feed_forward(
            current,
            gain,
            gate_weight,
            up_weight,
            down_weight,
            picked[0],
            picked[1],
            picked[2],
            picked[3],
            picked[4],
            picked[5],
        )
        valid = (position >= 0) & (position < block_count)
        before = output
        output = jnp.where(valid, result, before)
        if tick + 1 < ticks:
            arrived = from_behind(result, "pp", 1)
    pop_size = lax.axis_size("pop")
    population = members * pop_size
    all_ranks, all_gl, all_gr, all_ul, all_ur, all_dl, all_dr = (
        lax.all_gather(ranks, "pop", axis=0, tiled=True),
        *sent_together(
            (vectors[0], vectors[1], vectors[2], vectors[3], vectors[4], vectors[5]), "pop", 0, 1
        ),
    )
    fitness = (2.0 * all_ranks.astype(jnp.float32) / (population - 1) - 1.0) / math.sqrt(population)
    row_share = width // pop_size
    row_start = lax.axis_index("pop") * row_share
    own_gl = lax.dynamic_slice_in_dim(all_gl, row_start, row_share, 1)
    own_ul = lax.dynamic_slice_in_dim(all_ul, row_start, row_share, 1)
    own_dr = lax.dynamic_slice_in_dim(all_dr, row_start, row_share, 1)
    sum_gate = grouped_outer(fitness, own_gl, all_gr, pop_size)
    sum_up = grouped_outer(fitness, own_ul, all_ur, pop_size)
    sum_down = grouped_outer(fitness, all_dl, own_dr, pop_size)
    update_gate = sum_gate.astype(jnp.bfloat16)[None]
    update_up = sum_up.astype(jnp.bfloat16)[None]
    update_down = sum_down.astype(jnp.bfloat16)[None]
    return (output[None], update_gate, update_up, update_down)


def solution(mesh):
    placed = (
        P("tp", "pop", None),
        P("pp", None),
        P("pp", None, "tp"),
        P("pp", None, "tp"),
        P("pp", "tp", None),
        P("pp", "pop", None),
        P("pp", "pop", "tp"),
        P("pp", "pop", None),
        P("pp", "pop", "tp"),
        P("pp", "pop", "tp"),
        P("pp", "pop", None),
        P("pop"),
    )
    return jax.shard_map(
        per_device,
        mesh=mesh,
        in_specs=placed,
        out_specs=(
            P("pp", "tp", "pop", None),
            P("pp", "pop", "tp"),
            P("pp", "pop", "tp"),
            P("pp", "tp", "pop"),
        ),
        check_vma=False,
    )
```

profile of v0, /device:TPU:0, one launch (start us, length us, event | category | flops | bytes accessed | tf_op | source)
XLA Modules:
  0.0 329.0 jit_solution(4825222965416994438)
XLA Ops:
  7.2 1.3 fusion.20
  8.6 1.9 fusion.22
  10.5 0.7 bitcast_convert_fusion.1
  11.2 0.7 bitcast_convert_fusion
  12.0 53.0 %all-gather.4.cloned.1.call-done = bf16[256,2,4096]{2,0,1:T(8,128)(2,1)} async-done(((bf16[16,2,4096]{2,0,1:T(8,128)(2,1)}), bf16[256,2,4096]{2,0,1:T(8,128)(2,1)}) %all-gather.4.cloned.1.call-update) | async-done | bytes 4194320 | tf_op jit(solution)/shard_map/all_gather | solution.py:47
  64.9 3.5 %fusion.32 = f32[2,1,256]{2,1,0:T(1,128)S(1)} fusion(bf16[256,2,4096]{2,0,1:T(8,128)(2,1)} %all-gather.4.cloned.1.call-done, bf16[2,4096,1]{1,0,2:T(2,128)(2,1)} %bitcast.111), kind=kOutput, calls=%fused_computation.41 | convolution fusion | flops 4194304 | bytes 4212736 | tf_op jit(solution)/shard_map/rkd,kd->rk/dot_general | solution.py:52
  68.5 1.2 fusion.36
  69.7 5.6 %fusion.6 = f32[256,2,768]{2,0,1:T(8,128)S(1)} fusion(bf16[256,2,4096]{2,0,1:T(8,128)(2,1)S(1)} %copy-done, bf16[1,4096,768]{2,1,0:T(8,128)(2,1)} %param.15), kind=kOutput, calls=%fused_computation.8 | convolution fusion | flops 3221225472 | bytes 12058624 | tf_op jit(solution)/shard_map/rkd,df->rkf/dot_general | solution.py:51
  75.4 3.6 %multiply_convert_fusion.1 = bf16[256,2,768]{2,0,1:T(8,128)(2,1)S(1)} fusion(f32[256,2,768]{2,0,1:T(8,128)S(1)} %fusion.6, bf16[256,2,4096]{2,0,1:T(8,128)(2,1)S(1)} %copy-done, bf16[1,4096,768]{2,1,0:T(8,128)(2,1)S(1)} %bitcast.119, f32[2,768]{1,0:T(2,128)S(1)} %get-tuple-element.20, f32[256,2]{0,1:T(2,128)S(1)} %get-tuple-element.22, ...), kind=kOutput, calls=%fused_computation.18 | convolution fusion | flops 3225157632 | bytes 12861440 | tf_op jit(solution)/shard_map/rkd,df->rkf/dot_general | solution.py:48
  79.4 5.0 %add_convert_fusion.1 = bf16[256,2,4096]{2,0,1:T(8,128)(2,1)} fusion(bf16[256,2,768]{2,0,1:T(8,128)(2,1)S(1)} %multiply_convert_fusion.1, bf16[1,768,4096]{2,1,0:T(8,128)(2,1)S(1)} %bitcast.123, f32[2,4096]{1,0:T(2,128)S(1)} %bitcast_convert_fusion, f32[256,2]{0,1:T(2,128)S(1)} %fusion.45), kind=kOutput, calls=%fused_computation.1 | convolution fusion | flops 3227516928 | bytes 11307008 | tf_op jit(solution)/shard_map/rkf,fd->rkd/dot_general | solution.py:55
  84.5 77.5 %reduce-scatter.3.cloned.1.call-done = bf16[16,2,4096]{2,0,1:T(8,128)(2,1)} async-done(((bf16[256,2,4096]{2,0,1:T(8,128)(2,1)}), bf16[16,2,4096]{2,0,1:T(8,128)(2,1)}) %reduce-scatter.3.cloned.1.call-update) | async-done | bytes 262160 | tf_op jit(solution)/shard_map/reduce_scatter | solution.py:57
  162.0 1.1 fusion.23
  163.2 3.4 %collective-permute-start = (bf16[16,2,4096]{2,0,1:T(8,128)(2,1)S(1)}, bf16[16,2,4096]{2,0,1:T(8,128)(2,1)S(1)}, u32[]{:S(2)}, u32[]{:S(2)}) collective-permute-start(bf16[16,2,4096]{2,0,1:T(8,128)(2,1)S(1)} %fusion.23), channel_id=1, source_target_pairs={{0,1},{2,3},{4,5},{6,7},{8,9},{10,11},{12,13},{14,15},{16,17},{18,... | collective-permute-start | bytes 786440 | tf_op jit(solution)/shard_map/ppermute | solution.py:14
  166.5 3.9 %collective-permute-done = bf16[16,2,4096]{2,0,1:T(8,128)(2,1)S(1)} collective-permute-done((bf16[16,2,4096]{2,0,1:T(8,128)(2,1)S(1)}, bf16[16,2,4096]{2,0,1:T(8,128)(2,1)S(1)}, u32[]{:S(2)}, u32[]{:S(2)}) %collective-permute-start) | collective-permute-done | bytes 262176 | tf_op jit(solution)/shard_map/ppermute | solution.py:14
  170.6 0.8 fusion.26
  171.7 51.6 %all-gather.6.cloned.1.call-done = bf16[256,2,4096]{2,0,1:T(8,128)(2,1)} async-done(((bf16[16,2,4096]{2,0,1:T(8,128)(2,1)}), bf16[256,2,4096]{2,0,1:T(8,128)(2,1)}) %all-gather.6.cloned.1.call-update) | async-done | bytes 4194320 | tf_op jit(solution)/shard_map/all_gather | solution.py:47
  223.4 3.5 %fusion.30 = f32[2,1,256]{2,1,0:T(1,128)S(1)} fusion(bf16[256,2,4096]{2,0,1:T(8,128)(2,1)} %all-gather.6.cloned.1.call-done, bf16[2,4096,1]{1,0,2:T(2,128)(2,1)S(1)} %bitcast.112), kind=kOutput, calls=%fused_computation.39 | convolution fusion | flops 4194304 | bytes 4212736 | tf_op jit(solution)/shard_map/rkd,kd->rk/dot_general | solution.py:52
  226.9 1.2 fusion.34
  228.1 5.6 %fusion.4 = f32[256,2,768]{2,0,1:T(8,128)S(1)} fusion(bf16[256,2,4096]{2,0,1:T(8,128)(2,1)S(1)} %copy-done.1, bf16[1,4096,768]{2,1,0:T(8,128)(2,1)} %param.15), kind=kOutput, calls=%fused_computation.6 | convolution fusion | flops 3221225472 | bytes 12058624 | tf_op jit(solution)/shard_map/rkd,df->rkf/dot_general | solution.py:51
  233.8 3.6 %multiply_convert_fusion = bf16[256,2,768]{2,0,1:T(8,128)(2,1)S(1)} fusion(f32[256,2,768]{2,0,1:T(8,128)S(1)} %fusion.4, bf16[256,2,4096]{2,0,1:T(8,128)(2,1)S(1)} %copy-done.1, bf16[1,4096,768]{2,1,0:T(8,128)(2,1)S(1)} %bitcast.121, f32[256,2]{0,1:T(2,128)S(1)} %fusion.43, f32[256,2]{0,1:T(2,128)S(1)} %fusion.44, f32[2,768]{1,0:T(2,128)S(1)} %get-tuple-element.20, ...), kind=kOutput, calls=%fused_computation.17 | convolution fusion | flops 3225157632 | bytes 12861440 | tf_op jit(solution)/shard_map/rkd,df->rkf/dot_general | solution.py:48
  237.8 5.0 %add_convert_fusion = bf16[256,2,4096]{2,0,1:T(8,128)(2,1)} fusion(bf16[256,2,768]{2,0,1:T(8,128)(2,1)S(1)} %multiply_convert_fusion, bf16[1,768,4096]{2,1,0:T(8,128)(2,1)S(1)} %bitcast.125, f32[256,2]{0,1:T(2,128)S(1)} %fusion.42, f32[2,4096]{1,0:T(2,128)S(1)} %bitcast_convert_fusion), kind=kOutput, calls=%fused_computation | convolution fusion | flops 3227516928 | bytes 11307008 | tf_op jit(solution)/shard_map/rkf,fd->rkd/dot_general | solution.py:55
  245.0 6.4 %all-reduce = s32[8]{0:T(128)S(1)} all-reduce(s32[8]{0:T(128)S(1)} %dynamic-update-slice), channel_id=1, replica_groups=mesh['pop'=4,'tp'=16,'pp'=2] {'pop'}, use_global_device_ids=true, to_apply=%add | all-reduce | flops 8 | bytes 64
  251.5 7.4 %all-gather = bf16[4,2,14592]{2,1,0:T(2,128)(2,1)S(1)} all-gather(bf16[1,2,14592]{2,1,0:T(2,128)(2,1)S(1)} %bitcast.113), channel_id=1, replica_groups=mesh['pop'=4,'tp'=16,'pp'=2] {'pop'}, dimensions={0}, use_global_device_ids=true | all-gather | bytes 291840 | tf_op jit(solution)/shard_map/all_gather | solution.py:19
  259.4 4.5 %fusion.49 = bf16[4,768,1024]{2,1,0:T(8,128)(2,1)} fusion(bf16[4,2,768]{2,1,0:T(2,128)(2,1)S(1)} %reshape.60, bf16[4,2,1024]{2,1,0:T(2,128)(2,1)S(1)} %reshape.61), kind=kOutput, calls=%fused_computation.78 | convolution fusion | flops 12582912 | bytes 6320128 | tf_op jit(solution)/shard_map/gmi,gmj->gij/dot_general | solution.py:69
  263.8 4.5 %fusion.51 = bf16[4,1024,768]{2,1,0:T(8,128)(2,1)} fusion(bf16[4,2,1024]{2,1,0:T(2,128)(2,1)S(1)} %reshape.56, bf16[4,2,768]{2,1,0:T(2,128)(2,1)S(1)} %reshape.57), kind=kOutput, calls=%fused_computation.80 | convolution fusion | flops 12582912 | bytes 6320128 | tf_op jit(solution)/shard_map/gmi,gmj->gij/dot_general | solution.py:69
  268.3 6.0 %reduce_sum.58 = bf16[768,1024]{1,0:T(8,128)(2,1)} reduce(bf16[4,768,1024]{2,1,0:T(8,128)(2,1)} %fusion.49, bf16[]{:T(256)} %constant.15.clone.1), dimensions={0}, to_apply=%region_6.7 | reduce | flops 2359296 | bytes 7864322 | tf_op jit(solution)/shard_map/reduce_sum | solution.py:71
  274.3 5.4 %reduce_sum.56 = bf16[1024,768]{1,0:T(8,128)(2,1)} reduce(bf16[4,1024,768]{2,1,0:T(8,128)(2,1)} %fusion.51, bf16[]{:T(256)} %constant.15.clone.1), dimensions={0}, to_apply=%region_4.5 | reduce | flops 2359296 | bytes 7864322 | tf_op jit(solution)/shard_map/reduce_sum | solution.py:71
  279.7 4.5 %fusion.50 = bf16[4,1024,768]{2,1,0:T(8,128)(2,1)} fusion(bf16[4,2,1024]{2,1,0:T(2,128)(2,1)S(1)} %reshape.58, bf16[4,2,768]{2,1,0:T(2,128)(2,1)S(1)} %reshape.59), kind=kOutput, calls=%fused_computation.79 | convolution fusion | flops 12582912 | bytes 6320128 | tf_op jit(solution)/shard_map/gmi,gmj->gij/dot_general | solution.py:69
  284.2 5.3 %reduce_sum.57 = bf16[1024,768]{1,0:T(8,128)(2,1)} reduce(bf16[4,1024,768]{2,1,0:T(8,128)(2,1)} %fusion.50, bf16[]{:T(256)} %constant.15.clone.1), dimensions={0}, to_apply=%region_5.6 | reduce | flops 2359296 | bytes 7864322 | tf_op jit(solution)/shard_map/reduce_sum | solution.py:71
  289.5 30.8 %reduce-scatter.5.cloned.1.call-done = bf16[16,2,4096]{2,0,1:T(8,128)(2,1)} async-done(((bf16[256,2,4096]{2,0,1:T(8,128)(2,1)}), bf16[16,2,4096]{2,0,1:T(8,128)(2,1)}) %reduce-scatter.5.cloned.1.call-update) | async-done | bytes 262160 | tf_op jit(solution)/shard_map/reduce_scatter | solution.py:57
  320.4 1.1 fusion.29
  321.5 1.0 copy.19
  (82 shorter events, 3.2 us)
Async XLA Ops:
  7.2 61.3 %copy-start.3 = (bf16[1,2,4096]{2,1,0:T(2,128)(2,1)S(1)}, bf16[1,2,4096]{2,1,0:T(2,128)(2,1)}, u32[]{:S(2)}) copy-start(bf16[1,2,4096]{2,1,0:T(2,128)(2,1)} %param.17) | copy-start | bytes 49156
  7.2 57.8 %all-gather.4.cloned.1.call-start = ((), (), s32[]{:S(2)}) async-start(), calls=%async_computation.2 | async-start | bytes 4456448 | tf_op jit(solution)/shard_map/all_gather | solution.py:47
  10.5 151.6 %reduce-scatter.3.cloned.1.call-start = ((), (), s32[]{:S(2)}) async-start(), calls=%async_computation.3 | async-start | bytes 4456448 | tf_op jit(solution)/shard_map/reduce_scatter | solution.py:57
  64.9 3.5 %copy-start = (bf16[256,2,4096]{2,0,1:T(8,128)(2,1)S(1)}, bf16[256,2,4096]{2,0,1:T(8,128)(2,1)}, u32[]{:S(2)}) copy-start(bf16[256,2,4096]{2,0,1:T(8,128)(2,1)} %all-gather.4.cloned.1.call-done) | copy-start | bytes 12582916
  68.5 6.9 %slice-start = ((s8[6291456]{0:T(1024)(128)(4,1)}), s8[4194304]{0:T(1024)(128)(4,1)S(1)}, s32[]{:S(2)}) async-start(s8[6291456]{0:T(1024)(128)(4,1)} %bitcast.118), calls=%async_computation.6 | async-start | bytes 8388608
  69.7 5.7 %slice-start.1 = ((s8[6291456]{0:T(1024)(128)(4,1)}), s8[2097152]{0:T(1024)(128)(4,1)S(1)}, s32[]{:S(2)}) async-start(s8[6291456]{0:T(1024)(128)(4,1)} %bitcast.118), calls=%async_computation.7 | async-start | bytes 4194304
  69.7 9.7 %slice-start.4 = ((s8[6291456]{0:T(1024)(128)(4,1)}), s8[4194304]{0:T(1024)(128)(4,1)S(1)}, s32[]{:S(2)}) async-start(s8[6291456]{0:T(1024)(128)(4,1)} %bitcast.122), calls=%async_computation.10 | async-start | bytes 8388608
  75.4 3.7 %copy-start.5 = (bf16[1,2,768]{2,1,0:T(2,128)(2,1)S(1)}, bf16[1,2,768]{2,1,0:T(2,128)(2,1)}, u32[]{:S(2)}) copy-start(bf16[1,2,768]{2,1,0:T(2,128)(2,1)} %param.21) | copy-start | bytes 9220
  75.4 4.0 %slice-start.5 = ((s8[6291456]{0:T(1024)(128)(4,1)}), s8[2097152]{0:T(1024)(128)(4,1)S(1)}, s32[]{:S(2)}) async-start(s8[6291456]{0:T(1024)(128)(4,1)} %bitcast.122), calls=%async_computation.11 | async-start | bytes 4194304
  84.4 77.6 %copy-start.2 = (bf16[16,2,4096]{2,1,0:T(2,128)(2,1)S(1)}, bf16[16,2,4096]{2,1,0:T(2,128)(2,1)}, u32[]{:S(2)}) copy-start(bf16[16,2,4096]{2,1,0:T(2,128)(2,1)} %param.12) | copy-start | bytes 786436
  84.4 86.2 %copy-start.6 = (f32[1,4096]{1,0:T(1,128)S(1)}, f32[1,4096]{1,0:T(1,128)}, u32[]{:S(2)}) copy-start(f32[1,4096]{1,0:T(1,128)} %param.13) | copy-start | bytes 49156
  84.4 138.9 %copy-start.4 = (bf16[1,2,4096]{2,1,0:T(2,128)(2,1)S(1)}, bf16[1,2,4096]{2,1,0:T(2,128)(2,1)}, u32[]{:S(2)}) copy-start(bf16[1,2,4096]{2,1,0:T(2,128)(2,1)} %param.19) | copy-start | bytes 49156
  84.5 138.9 %all-gather.6.cloned.1.call-start = ((), (), s32[]{:S(2)}) async-start(), calls=%async_computation.4 | async-start | bytes 4456448 | tf_op jit(solution)/shard_map/all_gather | solution.py:47
  163.2 7.3 %collective-permute-start = (bf16[16,2,4096]{2,0,1:T(8,128)(2,1)S(1)}, bf16[16,2,4096]{2,0,1:T(8,128)(2,1)S(1)}, u32[]{:S(2)}, u32[]{:S(2)}) collective-permute-start(bf16[16,2,4096]{2,0,1:T(8,128)(2,1)S(1)} %fusion.23), channel_id=1, source_target_pairs={{0,1},{2,3},{4,5},{6,7},{8,9},{10,11},{12,13},{14,15},{16,17},{18,... | collective-permute-start | bytes 786440 | tf_op jit(solution)/shard_map/ppermute | solution.py:14
  171.5 148.9 %reduce-scatter.5.cloned.1.call-start = ((), (), s32[]{:S(2)}) async-start(), calls=%async_computation.5 | async-start | bytes 4456448 | tf_op jit(solution)/shard_map/reduce_scatter | solution.py:57
  223.4 3.5 %copy-start.1 = (bf16[256,2,4096]{2,0,1:T(8,128)(2,1)S(1)}, bf16[256,2,4096]{2,0,1:T(8,128)(2,1)}, u32[]{:S(2)}) copy-start(bf16[256,2,4096]{2,0,1:T(8,128)(2,1)} %all-gather.6.cloned.1.call-done) | copy-start | bytes 12582916
  226.9 6.9 %slice-start.2 = ((s8[6291456]{0:T(1024)(128)(4,1)}), s8[4194304]{0:T(1024)(128)(4,1)S(1)}, s32[]{:S(2)}) async-start(s8[6291456]{0:T(1024)(128)(4,1)} %bitcast.120), calls=%async_computation.8 | async-start | bytes 8388608
  228.1 5.7 %slice-start.3 = ((s8[6291456]{0:T(1024)(128)(4,1)}), s8[2097152]{0:T(1024)(128)(4,1)S(1)}, s32[]{:S(2)}) async-start(s8[6291456]{0:T(1024)(128)(4,1)} %bitcast.120), calls=%async_computation.9 | async-start | bytes 4194304
  228.1 9.7 %slice-start.6 = ((s8[6291456]{0:T(1024)(128)(4,1)}), s8[4194304]{0:T(1024)(128)(4,1)S(1)}, s32[]{:S(2)}) async-start(s8[6291456]{0:T(1024)(128)(4,1)} %bitcast.124), calls=%async_computation.12 | async-start | bytes 8388608
  233.8 4.0 %slice-start.7 = ((s8[6291456]{0:T(1024)(128)(4,1)}), s8[2097152]{0:T(1024)(128)(4,1)S(1)}, s32[]{:S(2)}) async-start(s8[6291456]{0:T(1024)(128)(4,1)} %bitcast.124), calls=%async_computation.13 | async-start | bytes 4194304
  242.8 0.7 copy-start.11
  242.8 1.9 copy-start.10
  242.8 8.6 %copy-start.8 = (bf16[1,2,768]{2,1,0:T(2,128)(2,1)S(1)}, bf16[1,2,768]{2,1,0:T(2,128)(2,1)}, u32[]{:S(2)}) copy-start(bf16[1,2,768]{2,1,0:T(2,128)(2,1)} %param.18) | copy-start | bytes 9220
  242.8 8.6 %copy-start.9 = (bf16[1,2,768]{2,1,0:T(2,128)(2,1)S(1)}, bf16[1,2,768]{2,1,0:T(2,128)(2,1)}, u32[]{:S(2)}) copy-start(bf16[1,2,768]{2,1,0:T(2,128)(2,1)} %param.20) | copy-start | bytes 9220
  242.8 8.7 %copy-start.7 = (bf16[1,2,4096]{2,1,0:T(2,128)(2,1)S(1)}, bf16[1,2,4096]{2,1,0:T(2,128)(2,1)}, u32[]{:S(2)}) copy-start(bf16[1,2,4096]{2,1,0:T(2,128)(2,1)} %param.22) | copy-start | bytes 49156
Sparse Core Ops, SparseCore 0:
  10.7 54.1 all-gather.3
  84.6 77.3 reduce-scatter.2
  171.6 51.7 all-gather.5
  243.0 77.3 reduce-scatter.4
where the time goes:
time: 329 us
  waiting for transfers between devices  217 us (66%)
  matrix products  52.1 us (16%)
  other arithmetic  24.7 us (8%)
  between operations  14.8 us (4%)
  blocking collectives  13.9 us (4%)
  starting transfers between devices  3.72 us (1%)
    reduce_scatter x2, waiting for transfers between devices, feed_forward(): lax.psum_scatter((term + coef_hidden * down_side[:, :, None] * down_wide)...  108 us
    all_gather x2, waiting for transfers between devices, feed_forward(): piece = lax.all_gather(normed, 'tp', axis=0, tiled=True)  105 us
    reduce_sum x3, other arithmetic, grouped_outer(): return jnp.sum(rounded, axis=0)  16.7 us
    dot_general x3, matrix products, grouped_outer(): parts = jnp.einsum('gmi,gmj->gij', weighted, other)  13.4 us
    dot_general x2, matrix products, feed_forward(): jnp.einsum('rkd,df->rkf', piece, w_up, preferred_element_type=jnp.float32)  11.3 us
    dot_general x2, matrix products, feed_forward(): jnp.einsum('rkf,fd->rkd', inner, w_down, preferred_element_type=jnp.float32)  10.1 us
    all_gather x1, blocking collectives, sent_together(): out, at, done = (lax.all_gather(both, axis, axis=dim, tiled=True), 0, [])  7.43 us
    dot_general x2, matrix products, feed_forward(): jnp.einsum('rkd,df->rkf', piece, w_gate, preferred_element_type=jnp.float32)  7.28 us
  transfers between devices with their start and end apart: 5, of which 5 were waited for; matrix products, arithmetic and copies ran while one was open for 10% of the time, Pallas kernels for 0%

commit v1 on v0

--- a/solution.py
+++ b/solution.py
@@ -44,7 +44,12 @@
     gate_wide = gate_right.astype(jnp.float32)[None]
     up_wide = up_right.astype(jnp.float32)[None]
     down_wide = down_right.astype(jnp.float32)[None]
-    piece = lax.all_gather(normed, "tp", axis=0, tiled=True)
+    ring = [normed]
+    for hop in range(15):
+        ring.append(lax.ppermute(ring[-1], "tp", [(dev, (dev + 1) % 16) for dev in range(16)]))
+    piece = jnp.roll(
+        jnp.concatenate(ring[::-1], axis=0), (lax.axis_index("tp") + 1) * ring[0].shape[0], axis=0
+    )
     gate = jnp.einsum("rkd,df->rkf", piece, w_gate, preferred_element_type=jnp.float32)
     gate_side = jnp.einsum("rkd,kd->rk", piece, gate_left, preferred_element_type=jnp.float32)
     gate = gate + coef_in * gate_side[:, :, None] * gate_wide

time: 329 us -> 539 us (1.64); the launches traced: 329 us -> 533 us
  waiting for transfers between devices: 217 us -> 416 us
  matrix products: 52.1 us -> 42.9 us
  other arithmetic: 24.7 us -> 30.8 us
    ppermute x0 -> x30, waiting for transfers between devices: none -> 309 us  [feed_forward(): lax.ppermute(ring[-1], 'tp', [(dev, (dev + 1) % 16) for dev in range(16)])]
    all_gather x2 -> x0, waiting for transfers between devices: 105 us -> none  [feed_forward(): piece = lax.all_gather(normed, 'tp', axis=0, tiled=True)]
    concatenate x0 -> x4, other arithmetic: none -> 7.17 us  [the longest x2 6.86 us: feed_forward(): jnp.roll(jnp.concatenate(ring[::-1], axis=0), (lax.axis_index('tp') + 1)...]
  transfers between devices with their start and end apart: 5 -> 33, of which waited for: 5 -> 33; matrix products, arithmetic and copies ran while one was open for 10% -> 6% of each run, Pallas kernels for 0% -> 0%
where the time goes in v1:
time: 539 us; the launch traced here: 533 us
  waiting for transfers between devices  416 us (77%)
  matrix products  42.9 us (8%)
  other arithmetic  30.8 us (6%)
  between operations  15.6 us (3%)
  blocking collectives  13.6 us (3%)
  starting transfers between devices  7.51 us (1%)
  local copies, waits for them, and re-layouts  6.99 us (1%)
    ppermute x30, waiting for transfers between devices, feed_forward(): lax.ppermute(ring[-1], 'tp', [(dev, (dev + 1) % 16) for dev in range(16)])  309 us
    reduce_scatter x2, waiting for transfers between devices, feed_forward(): lax.psum_scatter((term + coef_hidden * down_side[:, :, None] * down_wide)...  103 us
    reduce_sum x3, other arithmetic, grouped_outer(): return jnp.sum(rounded, axis=0)  16.9 us
    dot_general x3, matrix products, grouped_outer(): parts = jnp.einsum('gmi,gmj->gij', weighted, other)  13.6 us
  transfers between devices with their start and end apart: 33, of which 33 were waited for; matrix products, arithmetic and copies ran while one was open for 6% of the time, Pallas kernels for 0%

profile of v1, /device:TPU:0, one launch (start us, length us, event | category | flops | bytes accessed | tf_op | source)
XLA Modules:
  0.0 533.4 jit_solution(675826573306172142)
XLA Ops:
  11.4 11.0 %collective-permute-done = bf16[16,2,4096]{2,0,1:T(8,128)(2,1)S(1)} collective-permute-done((bf16[16,2,4096]{2,0,1:T(8,128)(2,1)S(1)}, bf16[16,2,4096]{2,0,1:T(8,128)(2,1)S(1)}, u32[]{:S(2)}, u32[]{:S(2)}) %collective-permute-start) | collective-permute-done | bytes 262176 | tf_op jit(solution)/shard_map/ppermute | solution.py:49
  22.5 10.8 %collective-permute-done.1 = bf16[16,2,4096]{2,0,1:T(8,128)(2,1)S(1)} collective-permute-done((bf16[16,2,4096]{2,0,1:T(8,128)(2,1)S(1)}, bf16[16,2,4096]{2,0,1:T(8,128)(2,1)S(1)}, u32[]{:S(2)}, u32[]{:S(2)}) %collective-permute-start.1) | collective-permute-done | bytes 262176 | tf_op jit(solution)/shard_map/ppermute | solution.py:49
  33.3 9.9 %collective-permute-done.2 = bf16[16,2,4096]{2,0,1:T(8,128)(2,1)S(1)} collective-permute-done((bf16[16,2,4096]{2,0,1:T(8,128)(2,1)S(1)}, bf16[16,2,4096]{2,0,1:T(8,128)(2,1)S(1)}, u32[]{:S(2)}, u32[]{:S(2)}) %collective-permute-start.2) | collective-permute-done | bytes 262176 | tf_op jit(solution)/shard_map/ppermute | solution.py:49
  43.2 9.7 %collective-permute-done.3 = bf16[16,2,4096]{2,0,1:T(8,128)(2,1)S(1)} collective-permute-done((bf16[16,2,4096]{2,0,1:T(8,128)(2,1)S(1)}, bf16[16,2,4096]{2,0,1:T(8,128)(2,1)S(1)}, u32[]{:S(2)}, u32[]{:S(2)}) %collective-permute-start.3) | collective-permute-done | bytes 262176 | tf_op jit(solution)/shard_map/ppermute | solution.py:49
  52.9 9.7 %collective-permute-done.4 = bf16[16,2,4096]{2,0,1:T(8,128)(2,1)S(1)} collective-permute-done((bf16[16,2,4096]{2,0,1:T(8,128)(2,1)S(1)}, bf16[16,2,4096]{2,0,1:T(8,128)(2,1)S(1)}, u32[]{:S(2)}, u32[]{:S(2)}) %collective-permute-start.4) | collective-permute-done | bytes 262176 | tf_op jit(solution)/shard_map/ppermute | solution.py:49
  62.6 9.7 %collective-permute-done.5 = bf16[16,2,4096]{2,0,1:T(8,128)(2,1)S(1)} collective-permute-done((bf16[16,2,4096]{2,0,1:T(8,128)(2,1)S(1)}, bf16[16,2,4096]{2,0,1:T(8,128)(2,1)S(1)}, u32[]{:S(2)}, u32[]{:S(2)}) %collective-permute-start.5) | collective-permute-done | bytes 262176 | tf_op jit(solution)/shard_map/ppermute | solution.py:49
  72.3 10.8 %collective-permute-done.6 = bf16[16,2,4096]{2,0,1:T(8,128)(2,1)S(1)} collective-permute-done((bf16[16,2,4096]{2,0,1:T(8,128)(2,1)S(1)}, bf16[16,2,4096]{2,0,1:T(8,128)(2,1)S(1)}, u32[]{:S(2)}, u32[]{:S(2)}) %collective-permute-start.6) | collective-permute-done | bytes 262176 | tf_op jit(solution)/shard_map/ppermute | solution.py:49
  83.1 12.0 %collective-permute-done.7 = bf16[16,2,4096]{2,0,1:T(8,128)(2,1)S(1)} collective-permute-done((bf16[16,2,4096]{2,0,1:T(8,128)(2,1)S(1)}, bf16[16,2,4096]{2,0,1:T(8,128)(2,1)S(1)}, u32[]{:S(2)}, u32[]{:S(2)}) %collective-permute-start.7) | collective-permute-done | bytes 262176 | tf_op jit(solution)/shard_map/ppermute | solution.py:49
  95.1 11.8 %collective-permute-done.8 = bf16[16,2,4096]{2,0,1:T(8,128)(2,1)S(1)} collective-permute-done((bf16[16,2,4096]{2,0,1:T(8,128)(2,1)S(1)}, bf16[16,2,4096]{2,0,1:T(8,128)(2,1)S(1)}, u32[]{:S(2)}, u32[]{:S(2)}) %collective-permute-start.8) | collective-permute-done | bytes 262176 | tf_op jit(solution)/shard_map/ppermute | solution.py:49
  106.9 11.0 %collective-permute-done.9 = bf16[16,2,4096]{2,0,1:T(8,128)(2,1)S(1)} collective-permute-done((bf16[16,2,4096]{2,0,1:T(8,128)(2,1)S(1)}, bf16[16,2,4096]{2,0,1:T(8,128)(2,1)S(1)}, u32[]{:S(2)}, u32[]{:S(2)}) %collective-permute-start.9) | collective-permute-done | bytes 262176 | tf_op jit(solution)/shard_map/ppermute | solution.py:49
  118.0 10.1 %collective-permute-done.10 = bf16[16,2,4096]{2,0,1:T(8,128)(2,1)S(1)} collective-permute-done((bf16[16,2,4096]{2,0,1:T(8,128)(2,1)S(1)}, bf16[16,2,4096]{2,0,1:T(8,128)(2,1)S(1)}, u32[]{:S(2)}, u32[]{:S(2)}) %collective-permute-start.10) | collective-permute-done | bytes 262176 | tf_op jit(solution)/shard_map/ppermute | solution.py:49
  128.1 9.7 %collective-permute-done.11 = bf16[16,2,4096]{2,0,1:T(8,128)(2,1)S(1)} collective-permute-done((bf16[16,2,4096]{2,0,1:T(8,128)(2,1)S(1)}, bf16[16,2,4096]{2,0,1:T(8,128)(2,1)S(1)}, u32[]{:S(2)}, u32[]{:S(2)}) %collective-permute-start.11) | collective-permute-done | bytes 262176 | tf_op jit(solution)/shard_map/ppermute | solution.py:49
  137.8 9.7 %collective-permute-done.12 = bf16[16,2,4096]{2,0,1:T(8,128)(2,1)S(1)} collective-permute-done((bf16[16,2,4096]{2,0,1:T(8,128)(2,1)S(1)}, bf16[16,2,4096]{2,0,1:T(8,128)(2,1)S(1)}, u32[]{:S(2)}, u32[]{:S(2)}) %collective-permute-start.12) | collective-permute-done | bytes 262176 | tf_op jit(solution)/shard_map/ppermute | solution.py:49
  148.2 9.8 %collective-permute-done.13 = bf16[16,2,4096]{2,0,1:T(8,128)(2,1)} collective-permute-done((bf16[16,2,4096]{2,0,1:T(8,128)(2,1)S(1)}, bf16[16,2,4096]{2,0,1:T(8,128)(2,1)}, u32[]{:S(2)}, u32[]{:S(2)}) %collective-permute-start.13) | collective-permute-done | bytes 262176 | tf_op jit(solution)/shard_map/ppermute | solution.py:49
  159.7 8.5 %collective-permute-done.14 = bf16[16,2,4096]{2,0,1:T(8,128)(2,1)} collective-permute-done((bf16[16,2,4096]{2,0,1:T(8,128)(2,1)}, bf16[16,2,4096]{2,0,1:T(8,128)(2,1)}, u32[]{:S(2)}, u32[]{:S(2)}) %collective-permute-start.14) | collective-permute-done | bytes 262176 | tf_op jit(solution)/shard_map/ppermute | solution.py:49
  190.1 74.3 %reduce-scatter.3.cloned.1.call-done = bf16[16,2,4096]{2,0,1:T(8,128)(2,1)} async-done(((bf16[256,2,4096]{2,0,1:T(8,128)(2,1)}), bf16[16,2,4096]{2,0,1:T(8,128)(2,1)}) %reduce-scatter.3.cloned.1.call-update) | async-done | bytes 262160 | tf_op jit(solution)/shard_map/reduce_scatter | solution.py:62
  275.0 8.4 %collective-permute-done.16 = bf16[16,2,4096]{2,0,1:T(8,128)(2,1)S(1)} collective-permute-done((bf16[16,2,4096]{2,0,1:T(8,128)(2,1)S(1)}, bf16[16,2,4096]{2,0,1:T(8,128)(2,1)S(1)}, u32[]{:S(2)}, u32[]{:S(2)}) %collective-permute-start.16) | collective-permute-done | bytes 262176 | tf_op jit(solution)/shard_map/ppermute | solution.py:49
  283.4 9.7 %collective-permute-done.17 = bf16[16,2,4096]{2,0,1:T(8,128)(2,1)S(1)} collective-permute-done((bf16[16,2,4096]{2,0,1:T(8,128)(2,1)S(1)}, bf16[16,2,4096]{2,0,1:T(8,128)(2,1)S(1)}, u32[]{:S(2)}, u32[]{:S(2)}) %collective-permute-start.17) | collective-permute-done | bytes 262176 | tf_op jit(solution)/shard_map/ppermute | solution.py:49
  293.1 9.8 %collective-permute-done.18 = bf16[16,2,4096]{2,0,1:T(8,128)(2,1)S(1)} collective-permute-done((bf16[16,2,4096]{2,0,1:T(8,128)(2,1)S(1)}, bf16[16,2,4096]{2,0,1:T(8,128)(2,1)S(1)}, u32[]{:S(2)}, u32[]{:S(2)}) %collective-permute-start.18) | collective-permute-done | bytes 262176 | tf_op jit(solution)/shard_map/ppermute | solution.py:49
  303.0 10.9 %collective-permute-done.19 = bf16[16,2,4096]{2,0,1:T(8,128)(2,1)S(1)} collective-permute-done((bf16[16,2,4096]{2,0,1:T(8,128)(2,1)S(1)}, bf16[16,2,4096]{2,0,1:T(8,128)(2,1)S(1)}, u32[]{:S(2)}, u32[]{:S(2)}) %collective-permute-start.19) | collective-permute-done | bytes 262176 | tf_op jit(solution)/shard_map/ppermute | solution.py:49
  313.9 12.2 %collective-permute-done.20 = bf16[16,2,4096]{2,0,1:T(8,128)(2,1)S(1)} collective-permute-done((bf16[16,2,4096]{2,0,1:T(8,128)(2,1)S(1)}, bf16[16,2,4096]{2,0,1:T(8,128)(2,1)S(1)}, u32[]{:S(2)}, u32[]{:S(2)}) %collective-permute-start.20) | collective-permute-done | bytes 262176 | tf_op jit(solution)/shard_map/ppermute | solution.py:49
  326.1 11.7 %collective-permute-done.21 = bf16[16,2,4096]{2,0,1:T(8,128)(2,1)S(1)} collective-permute-done((bf16[16,2,4096]{2,0,1:T(8,128)(2,1)S(1)}, bf16[16,2,4096]{2,0,1:T(8,128)(2,1)S(1)}, u32[]{:S(2)}, u32[]{:S(2)}) %collective-permute-start.21) | collective-permute-done | bytes 262176 | tf_op jit(solution)/shard_map/ppermute | solution.py:49
  337.8 10.9 %collective-permute-done.22 = bf16[16,2,4096]{2,0,1:T(8,128)(2,1)S(1)} collective-permute-done((bf16[16,2,4096]{2,0,1:T(8,128)(2,1)S(1)}, bf16[16,2,4096]{2,0,1:T(8,128)(2,1)S(1)}, u32[]{:S(2)}, u32[]{:S(2)}) %collective-permute-start.22) | collective-permute-done | bytes 262176 | tf_op jit(solution)/shard_map/ppermute | solution.py:49
  348.6 9.9 %collective-permute-done.23 = bf16[16,2,4096]{2,0,1:T(8,128)(2,1)S(1)} collective-permute-done((bf16[16,2,4096]{2,0,1:T(8,128)(2,1)S(1)}, bf16[16,2,4096]{2,0,1:T(8,128)(2,1)S(1)}, u32[]{:S(2)}, u32[]{:S(2)}) %collective-permute-start.23) | collective-permute-done | bytes 262176 | tf_op jit(solution)/shard_map/ppermute | solution.py:49
  358.6 9.7 %collective-permute-done.24 = bf16[16,2,4096]{2,0,1:T(8,128)(2,1)S(1)} collective-permute-done((bf16[16,2,4096]{2,0,1:T(8,128)(2,1)S(1)}, bf16[16,2,4096]{2,0,1:T(8,128)(2,1)S(1)}, u32[]{:S(2)}, u32[]{:S(2)}) %collective-permute-start.24) | collective-permute-done | bytes 262176 | tf_op jit(solution)/shard_map/ppermute | solution.py:49
  368.3 9.7 %collective-permute-done.25 = bf16[16,2,4096]{2,0,1:T(8,128)(2,1)S(1)} collective-permute-done((bf16[16,2,4096]{2,0,1:T(8,128)(2,1)S(1)}, bf16[16,2,4096]{2,0,1:T(8,128)(2,1)S(1)}, u32[]{:S(2)}, u32[]{:S(2)}) %collective-permute-start.25) | collective-permute-done | bytes 262176 | tf_op jit(solution)/shard_map/ppermute | solution.py:49
  378.0 9.7 %collective-permute-done.26 = bf16[16,2,4096]{2,0,1:T(8,128)(2,1)S(1)} collective-permute-done((bf16[16,2,4096]{2,0,1:T(8,128)(2,1)S(1)}, bf16[16,2,4096]{2,0,1:T(8,128)(2,1)S(1)}, u32[]{:S(2)}, u32[]{:S(2)}) %collective-permute-start.26) | collective-permute-done | bytes 262176 | tf_op jit(solution)/shard_map/ppermute | solution.py:49
  387.7 10.8 %collective-permute-done.27 = bf16[16,2,4096]{2,0,1:T(8,128)(2,1)S(1)} collective-permute-done((bf16[16,2,4096]{2,0,1:T(8,128)(2,1)S(1)}, bf16[16,2,4096]{2,0,1:T(8,128)(2,1)S(1)}, u32[]{:S(2)}, u32[]{:S(2)}) %collective-permute-start.27) | collective-permute-done | bytes 262176 | tf_op jit(solution)/shard_map/ppermute | solution.py:49
  398.4 11.8 %collective-permute-done.28 = bf16[16,2,4096]{2,0,1:T(8,128)(2,1)S(1)} collective-permute-done((bf16[16,2,4096]{2,0,1:T(8,128)(2,1)S(1)}, bf16[16,2,4096]{2,0,1:T(8,128)(2,1)S(1)}, u32[]{:S(2)}, u32[]{:S(2)}) %collective-permute-start.28) | collective-permute-done | bytes 262176 | tf_op jit(solution)/shard_map/ppermute | solution.py:49
  410.2 9.7 %collective-permute-done.29 = bf16[16,2,4096]{2,0,1:T(8,128)(2,1)S(1)} collective-permute-done((bf16[16,2,4096]{2,0,1:T(8,128)(2,1)S(1)}, bf16[16,2,4096]{2,0,1:T(8,128)(2,1)S(1)}, u32[]{:S(2)}, u32[]{:S(2)}) %collective-permute-start.29) | collective-permute-done | bytes 262176 | tf_op jit(solution)/shard_map/ppermute | solution.py:49
  420.1 9.7 %collective-permute-done.30 = bf16[16,2,4096]{2,0,1:T(8,128)(2,1)S(1)} collective-permute-done((bf16[16,2,4096]{2,0,1:T(8,128)(2,1)S(1)}, bf16[16,2,4096]{2,0,1:T(8,128)(2,1)S(1)}, u32[]{:S(2)}, u32[]{:S(2)}) %collective-permute-start.30) | collective-permute-done | bytes 262176 | tf_op jit(solution)/shard_map/ppermute | solution.py:49
  495.3 29.0 %reduce-scatter.5.cloned.1.call-done = bf16[16,2,4096]{2,0,1:T(8,128)(2,1)} async-done(((bf16[256,2,4096]{2,0,1:T(8,128)(2,1)}), bf16[16,2,4096]{2,0,1:T(8,128)(2,1)}) %reduce-scatter.5.cloned.1.call-update) | async-done | bytes 262160 | tf_op jit(solution)/shard_map/reduce_scatter | solution.py:62
  (178 shorter events, 105.7 us)
Async XLA Ops:
  7.2 257.3 %reduce-scatter.3.cloned.1.call-start = ((), (), s32[]{:S(2)}) async-start(), calls=%async_computation.2 | async-start | bytes 4456448 | tf_op jit(solution)/shard_map/reduce_scatter | solution.py:62
  9.8 12.7 %collective-permute-start = (bf16[16,2,4096]{2,0,1:T(8,128)(2,1)S(1)}, bf16[16,2,4096]{2,0,1:T(8,128)(2,1)S(1)}, u32[]{:S(2)}, u32[]{:S(2)}) collective-permute-start(bf16[16,2,4096]{2,0,1:T(8,128)(2,1)S(1)} %fusion.24), channel_id=1, source_target_pairs={{0,2},{2,4},{4,6},{6,8},{8,10},{10,12},{12,14},{14,16},{16,18},{18... | collective-permute-start | bytes 786440 | tf_op jit(solution)/shard_map/ppermute | solution.py:49
  22.5 10.8 %collective-permute-start.1 = (bf16[16,2,4096]{2,0,1:T(8,128)(2,1)S(1)}, bf16[16,2,4096]{2,0,1:T(8,128)(2,1)S(1)}, u32[]{:S(2)}, u32[]{:S(2)}) collective-permute-start(bf16[16,2,4096]{2,0,1:T(8,128)(2,1)S(1)} %collective-permute-done), channel_id=1, source_target_pairs={{0,2},{2,4},{4,6},{6,8},{8,10},{10,12},{12,14},{14,16},{16,18},{18... | collective-permute-start | bytes 786440 | tf_op jit(solution)/shard_map/ppermute | solution.py:49
  33.3 9.9 %collective-permute-start.2 = (bf16[16,2,4096]{2,0,1:T(8,128)(2,1)S(1)}, bf16[16,2,4096]{2,0,1:T(8,128)(2,1)S(1)}, u32[]{:S(2)}, u32[]{:S(2)}) collective-permute-start(bf16[16,2,4096]{2,0,1:T(8,128)(2,1)S(1)} %collective-permute-done.1), channel_id=1, source_target_pairs={{0,2},{2,4},{4,6},{6,8},{8,10},{10,12},{12,14},{14,16},{16,18},{18... | collective-permute-start | bytes 786440 | tf_op jit(solution)/shard_map/ppermute | solution.py:49
  43.2 9.7 %collective-permute-start.3 = (bf16[16,2,4096]{2,0,1:T(8,128)(2,1)S(1)}, bf16[16,2,4096]{2,0,1:T(8,128)(2,1)S(1)}, u32[]{:S(2)}, u32[]{:S(2)}) collective-permute-start(bf16[16,2,4096]{2,0,1:T(8,128)(2,1)S(1)} %collective-permute-done.2), channel_id=1, source_target_pairs={{0,2},{2,4},{4,6},{6,8},{8,10},{10,12},{12,14},{14,16},{16,18},{18... | collective-permute-start | bytes 786440 | tf_op jit(solution)/shard_map/ppermute | solution.py:49
  52.9 9.7 %collective-permute-start.4 = (bf16[16,2,4096]{2,0,1:T(8,128)(2,1)S(1)}, bf16[16,2,4096]{2,0,1:T(8,128)(2,1)S(1)}, u32[]{:S(2)}, u32[]{:S(2)}) collective-permute-start(bf16[16,2,4096]{2,0,1:T(8,128)(2,1)S(1)} %collective-permute-done.3), channel_id=1, source_target_pairs={{0,2},{2,4},{4,6},{6,8},{8,10},{10,12},{12,14},{14,16},{16,18},{18... | collective-permute-start | bytes 786440 | tf_op jit(solution)/shard_map/ppermute | solution.py:49
  62.6 9.7 %collective-permute-start.5 = (bf16[16,2,4096]{2,0,1:T(8,128)(2,1)S(1)}, bf16[16,2,4096]{2,0,1:T(8,128)(2,1)S(1)}, u32[]{:S(2)}, u32[]{:S(2)}) collective-permute-start(bf16[16,2,4096]{2,0,1:T(8,128)(2,1)S(1)} %collective-permute-done.4), channel_id=1, source_target_pairs={{0,2},{2,4},{4,6},{6,8},{8,10},{10,12},{12,14},{14,16},{16,18},{18... | collective-permute-start | bytes 786440 | tf_op jit(solution)/shard_map/ppermute | solution.py:49
  72.3 10.8 %collective-permute-start.6 = (bf16[16,2,4096]{2,0,1:T(8,128)(2,1)S(1)}, bf16[16,2,4096]{2,0,1:T(8,128)(2,1)S(1)}, u32[]{:S(2)}, u32[]{:S(2)}) collective-permute-start(bf16[16,2,4096]{2,0,1:T(8,128)(2,1)S(1)} %collective-permute-done.5), channel_id=1, source_target_pairs={{0,2},{2,4},{4,6},{6,8},{8,10},{10,12},{12,14},{14,16},{16,18},{18... | collective-permute-start | bytes 786440 | tf_op jit(solution)/shard_map/ppermute | solution.py:49
  83.1 12.0 %collective-permute-start.7 = (bf16[16,2,4096]{2,0,1:T(8,128)(2,1)S(1)}, bf16[16,2,4096]{2,0,1:T(8,128)(2,1)S(1)}, u32[]{:S(2)}, u32[]{:S(2)}) collective-permute-start(bf16[16,2,4096]{2,0,1:T(8,128)(2,1)S(1)} %collective-permute-done.6), channel_id=1, source_target_pairs={{0,2},{2,4},{4,6},{6,8},{8,10},{10,12},{12,14},{14,16},{16,18},{18... | collective-permute-start | bytes 786440 | tf_op jit(solution)/shard_map/ppermute | solution.py:49
  95.1 11.8 %collective-permute-start.8 = (bf16[16,2,4096]{2,0,1:T(8,128)(2,1)S(1)}, bf16[16,2,4096]{2,0,1:T(8,128)(2,1)S(1)}, u32[]{:S(2)}, u32[]{:S(2)}) collective-permute-start(bf16[16,2,4096]{2,0,1:T(8,128)(2,1)S(1)} %collective-permute-done.7), channel_id=1, source_target_pairs={{0,2},{2,4},{4,6},{6,8},{8,10},{10,12},{12,14},{14,16},{16,18},{18... | collective-permute-start | bytes 786440 | tf_op jit(solution)/shard_map/ppermute | solution.py:49
  106.9 11.0 %collective-permute-start.9 = (bf16[16,2,4096]{2,0,1:T(8,128)(2,1)S(1)}, bf16[16,2,4096]{2,0,1:T(8,128)(2,1)S(1)}, u32[]{:S(2)}, u32[]{:S(2)}) collective-permute-start(bf16[16,2,4096]{2,0,1:T(8,128)(2,1)S(1)} %collective-permute-done.8), channel_id=1, source_target_pairs={{0,2},{2,4},{4,6},{6,8},{8,10},{10,12},{12,14},{14,16},{16,18},{18... | collective-permute-start | bytes 786440 | tf_op jit(solution)/shard_map/ppermute | solution.py:49
  118.0 10.1 %collective-permute-start.10 = (bf16[16,2,4096]{2,0,1:T(8,128)(2,1)S(1)}, bf16[16,2,4096]{2,0,1:T(8,128)(2,1)S(1)}, u32[]{:S(2)}, u32[]{:S(2)}) collective-permute-start(bf16[16,2,4096]{2,0,1:T(8,128)(2,1)S(1)} %collective-permute-done.9), channel_id=1, source_target_pairs={{0,2},{2,4},{4,6},{6,8},{8,10},{10,12},{12,14},{14,16},{16,18},{18... | collective-permute-start | bytes 786440 | tf_op jit(solution)/shard_map/ppermute | solution.py:49
  128.1 9.7 %collective-permute-start.11 = (bf16[16,2,4096]{2,0,1:T(8,128)(2,1)S(1)}, bf16[16,2,4096]{2,0,1:T(8,128)(2,1)S(1)}, u32[]{:S(2)}, u32[]{:S(2)}) collective-permute-start(bf16[16,2,4096]{2,0,1:T(8,128)(2,1)S(1)} %collective-permute-done.10), channel_id=1, source_target_pairs={{0,2},{2,4},{4,6},{6,8},{8,10},{10,12},{12,14},{14,16},{16,18},{18... | collective-permute-start | bytes 786440 | tf_op jit(solution)/shard_map/ppermute | solution.py:49
  137.8 9.7 %collective-permute-start.12 = (bf16[16,2,4096]{2,0,1:T(8,128)(2,1)S(1)}, bf16[16,2,4096]{2,0,1:T(8,128)(2,1)S(1)}, u32[]{:S(2)}, u32[]{:S(2)}) collective-permute-start(bf16[16,2,4096]{2,0,1:T(8,128)(2,1)S(1)} %collective-permute-done.11), channel_id=1, source_target_pairs={{0,2},{2,4},{4,6},{6,8},{8,10},{10,12},{12,14},{14,16},{16,18},{18... | collective-permute-start | bytes 786440 | tf_op jit(solution)/shard_map/ppermute | solution.py:49
  148.2 9.8 %collective-permute-start.13 = (bf16[16,2,4096]{2,0,1:T(8,128)(2,1)S(1)}, bf16[16,2,4096]{2,0,1:T(8,128)(2,1)}, u32[]{:S(2)}, u32[]{:S(2)}) collective-permute-start(bf16[16,2,4096]{2,0,1:T(8,128)(2,1)S(1)} %collective-permute-done.12), channel_id=1, source_target_pairs={{0,2},{2,4},{4,6},{6,8},{8,10},{10,12},{12,14},{14,16},{16,18},{18... | collective-permute-start | bytes 786440 | tf_op jit(solution)/shard_map/ppermute | solution.py:49
  158.0 10.3 %collective-permute-start.14 = (bf16[16,2,4096]{2,0,1:T(8,128)(2,1)}, bf16[16,2,4096]{2,0,1:T(8,128)(2,1)}, u32[]{:S(2)}, u32[]{:S(2)}) collective-permute-start(bf16[16,2,4096]{2,0,1:T(8,128)(2,1)} %collective-permute-done.13), channel_id=1, source_target_pairs={{0,2},{2,4},{4,6},{6,8},{8,10},{10,12},{12,14},{14,16},{16,18},{18... | collective-permute-start | bytes 786440 | tf_op jit(solution)/shard_map/ppermute | solution.py:49
  190.1 334.2 %reduce-scatter.5.cloned.1.call-start = ((), (), s32[]{:S(2)}) async-start(), calls=%async_computation.3 | async-start | bytes 4456448 | tf_op jit(solution)/shard_map/reduce_scatter | solution.py:62
  273.2 10.3 %collective-permute-start.16 = (bf16[16,2,4096]{2,0,1:T(8,128)(2,1)S(1)}, bf16[16,2,4096]{2,0,1:T(8,128)(2,1)S(1)}, u32[]{:S(2)}, u32[]{:S(2)}) collective-permute-start(bf16[16,2,4096]{2,0,1:T(8,128)(2,1)S(1)} %fusion.28), channel_id=1, source_target_pairs={{0,2},{2,4},{4,6},{6,8},{8,10},{10,12},{12,14},{14,16},{16,18},{18... | collective-permute-start | bytes 786440 | tf_op jit(solution)/shard_map/ppermute | solution.py:49
  283.4 9.7 %collective-permute-start.17 = (bf16[16,2,4096]{2,0,1:T(8,128)(2,1)S(1)}, bf16[16,2,4096]{2,0,1:T(8,128)(2,1)S(1)}, u32[]{:S(2)}, u32[]{:S(2)}) collective-permute-start(bf16[16,2,4096]{2,0,1:T(8,128)(2,1)S(1)} %collective-permute-done.16), channel_id=1, source_target_pairs={{0,2},{2,4},{4,6},{6,8},{8,10},{10,12},{12,14},{14,16},{16,18},{18... | collective-permute-start | bytes 786440 | tf_op jit(solution)/shard_map/ppermute | solution.py:49
  293.1 9.9 %collective-permute-start.18 = (bf16[16,2,4096]{2,0,1:T(8,128)(2,1)S(1)}, bf16[16,2,4096]{2,0,1:T(8,128)(2,1)S(1)}, u32[]{:S(2)}, u32[]{:S(2)}) collective-permute-start(bf16[16,2,4096]{2,0,1:T(8,128)(2,1)S(1)} %collective-permute-done.17), channel_id=1, source_target_pairs={{0,2},{2,4},{4,6},{6,8},{8,10},{10,12},{12,14},{14,16},{16,18},{18... | collective-permute-start | bytes 786440 | tf_op jit(solution)/shard_map/ppermute | solution.py:49
  303.0 10.9 %collective-permute-start.19 = (bf16[16,2,4096]{2,0,1:T(8,128)(2,1)S(1)}, bf16[16,2,4096]{2,0,1:T(8,128)(2,1)S(1)}, u32[]{:S(2)}, u32[]{:S(2)}) collective-permute-start(bf16[16,2,4096]{2,0,1:T(8,128)(2,1)S(1)} %collective-permute-done.18), channel_id=1, source_target_pairs={{0,2},{2,4},{4,6},{6,8},{8,10},{10,12},{12,14},{14,16},{16,18},{18... | collective-permute-start | bytes 786440 | tf_op jit(solution)/shard_map/ppermute | solution.py:49
  313.9 12.2 %collective-permute-start.20 = (bf16[16,2,4096]{2,0,1:T(8,128)(2,1)S(1)}, bf16[16,2,4096]{2,0,1:T(8,128)(2,1)S(1)}, u32[]{:S(2)}, u32[]{:S(2)}) collective-permute-start(bf16[16,2,4096]{2,0,1:T(8,128)(2,1)S(1)} %collective-permute-done.19), channel_id=1, source_target_pairs={{0,2},{2,4},{4,6},{6,8},{8,10},{10,12},{12,14},{14,16},{16,18},{18... | collective-permute-start | bytes 786440 | tf_op jit(solution)/shard_map/ppermute | solution.py:49
  326.1 11.7 %collective-permute-start.21 = (bf16[16,2,4096]{2,0,1:T(8,128)(2,1)S(1)}, bf16[16,2,4096]{2,0,1:T(8,128)(2,1)S(1)}, u32[]{:S(2)}, u32[]{:S(2)}) collective-permute-start(bf16[16,2,4096]{2,0,1:T(8,128)(2,1)S(1)} %collective-permute-done.20), channel_id=1, source_target_pairs={{0,2},{2,4},{4,6},{6,8},{8,10},{10,12},{12,14},{14,16},{16,18},{18... | collective-permute-start | bytes 786440 | tf_op jit(solution)/shard_map/ppermute | solution.py:49
  337.8 10.9 %collective-permute-start.22 = (bf16[16,2,4096]{2,0,1:T(8,128)(2,1)S(1)}, bf16[16,2,4096]{2,0,1:T(8,128)(2,1)S(1)}, u32[]{:S(2)}, u32[]{:S(2)}) collective-permute-start(bf16[16,2,4096]{2,0,1:T(8,128)(2,1)S(1)} %collective-permute-done.21), channel_id=1, source_target_pairs={{0,2},{2,4},{4,6},{6,8},{8,10},{10,12},{12,14},{14,16},{16,18},{18... | collective-permute-start | bytes 786440 | tf_op jit(solution)/shard_map/ppermute | solution.py:49
  348.6 9.9 %collective-permute-start.23 = (bf16[16,2,4096]{2,0,1:T(8,128)(2,1)S(1)}, bf16[16,2,4096]{2,0,1:T(8,128)(2,1)S(1)}, u32[]{:S(2)}, u32[]{:S(2)}) collective-permute-start(bf16[16,2,4096]{2,0,1:T(8,128)(2,1)S(1)} %collective-permute-done.22), channel_id=1, source_target_pairs={{0,2},{2,4},{4,6},{6,8},{8,10},{10,12},{12,14},{14,16},{16,18},{18... | collective-permute-start | bytes 786440 | tf_op jit(solution)/shard_map/ppermute | solution.py:49
  358.6 9.7 %collective-permute-start.24 = (bf16[16,2,4096]{2,0,1:T(8,128)(2,1)S(1)}, bf16[16,2,4096]{2,0,1:T(8,128)(2,1)S(1)}, u32[]{:S(2)}, u32[]{:S(2)}) collective-permute-start(bf16[16,2,4096]{2,0,1:T(8,128)(2,1)S(1)} %collective-permute-done.23), channel_id=1, source_target_pairs={{0,2},{2,4},{4,6},{6,8},{8,10},{10,12},{12,14},{14,16},{16,18},{18... | collective-permute-start | bytes 786440 | tf_op jit(solution)/shard_map/ppermute | solution.py:49
  368.3 9.7 %collective-permute-start.25 = (bf16[16,2,4096]{2,0,1:T(8,128)(2,1)S(1)}, bf16[16,2,4096]{2,0,1:T(8,128)(2,1)S(1)}, u32[]{:S(2)}, u32[]{:S(2)}) collective-permute-start(bf16[16,2,4096]{2,0,1:T(8,128)(2,1)S(1)} %collective-permute-done.24), channel_id=1, source_target_pairs={{0,2},{2,4},{4,6},{6,8},{8,10},{10,12},{12,14},{14,16},{16,18},{18... | collective-permute-start | bytes 786440 | tf_op jit(solution)/shard_map/ppermute | solution.py:49
  378.0 9.7 %collective-permute-start.26 = (bf16[16,2,4096]{2,0,1:T(8,128)(2,1)S(1)}, bf16[16,2,4096]{2,0,1:T(8,128)(2,1)S(1)}, u32[]{:S(2)}, u32[]{:S(2)}) collective-permute-start(bf16[16,2,4096]{2,0,1:T(8,128)(2,1)S(1)} %collective-permute-done.25), channel_id=1, source_target_pairs={{0,2},{2,4},{4,6},{6,8},{8,10},{10,12},{12,14},{14,16},{16,18},{18... | collective-permute-start | bytes 786440 | tf_op jit(solution)/shard_map/ppermute | solution.py:49
  387.6 10.8 %collective-permute-start.27 = (bf16[16,2,4096]{2,0,1:T(8,128)(2,1)S(1)}, bf16[16,2,4096]{2,0,1:T(8,128)(2,1)S(1)}, u32[]{:S(2)}, u32[]{:S(2)}) collective-permute-start(bf16[16,2,4096]{2,0,1:T(8,128)(2,1)S(1)} %collective-permute-done.26), channel_id=1, source_target_pairs={{0,2},{2,4},{4,6},{6,8},{8,10},{10,12},{12,14},{14,16},{16,18},{18... | collective-permute-start | bytes 786440 | tf_op jit(solution)/shard_map/ppermute | solution.py:49
  398.4 11.8 %collective-permute-start.28 = (bf16[16,2,4096]{2,0,1:T(8,128)(2,1)S(1)}, bf16[16,2,4096]{2,0,1:T(8,128)(2,1)S(1)}, u32[]{:S(2)}, u32[]{:S(2)}) collective-permute-start(bf16[16,2,4096]{2,0,1:T(8,128)(2,1)S(1)} %collective-permute-done.27), channel_id=1, source_target_pairs={{0,2},{2,4},{4,6},{6,8},{8,10},{10,12},{12,14},{14,16},{16,18},{18... | collective-permute-start | bytes 786440 | tf_op jit(solution)/shard_map/ppermute | solution.py:49
  410.2 9.7 %collective-permute-start.29 = (bf16[16,2,4096]{2,0,1:T(8,128)(2,1)S(1)}, bf16[16,2,4096]{2,0,1:T(8,128)(2,1)S(1)}, u32[]{:S(2)}, u32[]{:S(2)}) collective-permute-start(bf16[16,2,4096]{2,0,1:T(8,128)(2,1)S(1)} %collective-permute-done.28), channel_id=1, source_target_pairs={{0,2},{2,4},{4,6},{6,8},{8,10},{10,12},{12,14},{14,16},{16,18},{18... | collective-permute-start | bytes 786440 | tf_op jit(solution)/shard_map/ppermute | solution.py:49
  419.9 9.8 %collective-permute-start.30 = (bf16[16,2,4096]{2,0,1:T(8,128)(2,1)S(1)}, bf16[16,2,4096]{2,0,1:T(8,128)(2,1)S(1)}, u32[]{:S(2)}, u32[]{:S(2)}) collective-permute-start(bf16[16,2,4096]{2,0,1:T(8,128)(2,1)S(1)} %collective-permute-done.29), channel_id=1, source_target_pairs={{0,2},{2,4},{4,6},{6,8},{8,10},{10,12},{12,14},{14,16},{16,18},{18... | collective-permute-start | bytes 786440 | tf_op jit(solution)/shard_map/ppermute | solution.py:49
  (24 other events, 429.0 us)
Sparse Core Ops, SparseCore 0:
  190.2 74.1 reduce-scatter.2
  448.7 75.5 reduce-scatter.4
